TPU v7x, 768 devices: a whole 4x8x12 slice. The times are simulated.
768 devices in a mesh: wave: 48 (over x, z), lat: 16 (over y, core).
Axes of the slice: x: 4, y: 8, z: 12, core: 2. Of those that a mesh axis runs over, the one named last changes fastest.
Arguments:
- legendre: bfloat16 [384, 384, 1536], P('wave', None, 'lat'), may hold values from -0.3125 to 0.3125
- coefficients: bfloat16 [384, 384, 128], P('wave', 'lat'), may hold values from -0.29882812 to 0.29882812
- assignment: int32 [384], replicated, may hold values from 0 to 383, as said below
Outputs:
- grid: float32 [16, 96, 64, 5120], P('lat', 'wave')
Inputs may be any that keep to these rules, and one draw needn't show every extreme that they name: assignment is a permutation of the 384 slab indices; storage rows 2 i and 2 i + 1 hold slab indices j and 383 - j.
All inputs are finite; a program needn't handle non-finite values.
Results may differ from a plain program's by a relative error of at most 0.0037.
Values may be sent and summed in bfloat16 or wider, within the bound.
No kernel may reach another device: no remote copies, remote signals or barrier semaphores. Data moves between devices by JAX's collectives and lax.ppermute only.
A program may use at most 64 MiB of HBM per device.

v0:
```python
import jax
import jax.numpy as jnp
from jax import lax
from jax.sharding import PartitionSpec as P

MTOP = 2559
C = 64
LONGITUDES = 5120


def build_table(assignment, all_rows):
    table_row = jnp.arange(2 * all_rows, dtype=jnp.int32)
    frequency = MTOP - all_rows + 1 + assignment[table_row // 2]
    longitude = jnp.arange(LONGITUDES, dtype=jnp.int32)
    phase_index = frequency[:, None] * longitude[None, :] % LONGITUDES
    angles = phase_index.astype(jnp.float32) * jnp.float32(2.0 * 3.141592653589793 / LONGITUDES)
    parity = (table_row % 2)[:, None] == 0
    dft_table = jnp.where(parity, 2.0 * jnp.cos(angles), -2.0 * jnp.sin(angles))
    return dft_table.astype(jnp.bfloat16)


def shards(legendre, coefficients, assignment):
    row_count = legendre.shape[0]
    lat_count = legendre.shape[2]
    deg_count = coefficients.shape[1]
    all_rows = assignment.shape[0]
    wave_count = lax.axis_size("wave")
    lat_rows = lat_count // wave_count
    wave_index = lax.axis_index("wave")
    lat_index = lax.axis_index("lat")
    own_waves = lax.dynamic_slice_in_dim(assignment, wave_index * row_count, row_count)
    degree = lat_index * deg_count + jnp.arange(deg_count, dtype=jnp.int32)
    keep_mask = degree[None, :] < (all_rows - own_waves)[:, None]
    masked = jnp.where(keep_mask[:, :, None], coefficients, jnp.zeros_like(coefficients))
    lat_sum = jnp.einsum(
        "rkl,rkc->lrc",
        legendre,
        lax.all_gather(masked, "lat", axis=1, tiled=True),
        preferred_element_type=jnp.float32,
    )
    fields = lat_sum.astype(jnp.bfloat16)
    dft_table = build_table(assignment, all_rows)
    by_dest = fields.reshape(wave_count, lat_rows, row_count, fields.shape[2])
    exchanged = lax.all_to_all(by_dest, "wave", split_axis=0, concat_axis=2, tiled=True)
    items = exchanged.shape[1]
    spectra_rows = exchanged.reshape(items, all_rows * 2, C)
    result = jnp.einsum("imc,mn->icn", spectra_rows, dft_table, preferred_element_type=jnp.float32)
    return result[None]


def solution(mesh):
    in_specs = (P("wave", None, "lat"), P("wave", "lat", None), P())
    out_specs = P("lat", "wave", None, None)
    return jax.shard_map(shards, mesh=mesh, in_specs=in_specs, out_specs=out_specs, check_vma=False)
```

profile of v0, /device:TPU:1, one launch (start us, length us, event | category | flops | bytes accessed | tf_op | source)
XLA Modules:
  0.0 126.8 jit_solution(14331332309411025871)
XLA Ops:
  0.0 0.0 copy-start
  0.0 0.0 copy-start.1
  0.0 0.8 dynamic-slice_subtract_fusion
  0.8 0.1 broadcast_compare_fusion
  0.9 0.9 broadcast_select_fusion
  1.8 27.2 %all_gather.3 = bf16[8,384,128]{2,1,0:T(8,128)(2,1)S(1)} all-gather(bf16[8,24,128]{2,1,0:T(8,128)(2,1)S(1)} %broadcast_select_fusion), channel_id=1, replica_groups=mesh['wave'=48,'lat'=16] {'lat'}, dimensions={1}, use_global_device_ids=true | all-gather | bytes 835584 | tf_op jit(solution)/shard_map/all_gather | solution.py:38
  29.0 0.0 copy-done
  29.0 0.3 convolution_convert_fusion
  29.3 0.8 copy.6
  30.1 11.9 %all-to-all-start = ((bf16[48,2,8,128]{3,2,1,0:T(8,128)(2,1)}), bf16[48,2,8,128]{3,2,1,0:T(8,128)(2,1)S(1)}, u32[]{:S(2)}, u32[]{:S(2)}) async-start(bf16[48,2,8,128]{3,2,1,0:T(8,128)(2,1)} %copy.6), calls=%async_computation | async-start | bytes 393216 | tf_op jit(solution)/shard_map/all_to_all | solution.py:44
  42.1 0.0 copy-done.1
  42.1 5.0 %gather_fusion = s32[768]{0:T(1024)S(1)} fusion(s32[384]{0:T(512)S(1)} %copy-done.1, s32[1024]{0:T(1024)S(1)} %pad_clamp_fusion), kind=kCustom, calls=%fused_computation | custom fusion | bytes 9216 | tf_op jit(solution)/shard_map/gather | solution.py:13
  47.1 9.5 %all-to-all-done = bf16[48,2,8,128]{3,2,1,0:T(8,128)(2,1)S(1)} async-done(((bf16[48,2,8,128]{3,2,1,0:T(8,128)(2,1)}), bf16[48,2,8,128]{3,2,1,0:T(8,128)(2,1)S(1)}, u32[]{:S(2)}, u32[]{:S(2)}) %all-to-all-start) | async-done | bytes 196640 | tf_op jit(solution)/shard_map/all_to_all | solution.py:44
  56.6 0.2 reshape.97
  56.8 70.0 %fusion.10 = f32[1,2,64,5120]{3,2,1,0:T(8,128)} fusion(bf16[2,768,64]{2,1,0:T(8,128)(2,1)S(1)} %reshape.97, s32[768]{0:T(1024)S(1)} %broadcast_add_fusion, pred[768]{0:T(1024)(128)(4,1)S(1)} %fusion.13), kind=kOutput, calls=%fused_computation.13 | convolution fusion | flops 1057751040 | bytes 2821888 | tf_op jit(solution)/shard_map/imc,mn->icn/dot_general | solution.py:47
  (6 shorter events, 0.1 us)
Async XLA Ops:
  0.0 29.0 %copy-start = (bf16[8,384,96]{1,2,0:T(8,128)(2,1)S(1)}, bf16[8,384,96]{1,2,0:T(8,128)(2,1)}, u32[]{:S(2)}) copy-start(bf16[8,384,96]{1,2,0:T(8,128)(2,1)} %param.3) | copy-start | bytes 1769476
  0.0 42.0 %copy-start.1 = (s32[384]{0:T(512)S(1)}, s32[384]{0:T(512)}, u32[]{:S(2)}) copy-start(s32[384]{0:T(512)} %param.5) | copy-start | bytes 4612
  30.1 26.5 %all-to-all-start = ((bf16[48,2,8,128]{3,2,1,0:T(8,128)(2,1)}), bf16[48,2,8,128]{3,2,1,0:T(8,128)(2,1)S(1)}, u32[]{:S(2)}, u32[]{:S(2)}) async-start(bf16[48,2,8,128]{3,2,1,0:T(8,128)(2,1)} %copy.6), calls=%async_computation | async-start | bytes 393216 | tf_op jit(solution)/shard_map/all_to_all | solution.py:44
where the time goes:
time: 127 us
  matrix products  70.4 us (55%)
  blocking collectives  27.2 us (21%)
  starting transfers between devices  11.9 us (9%)
  waiting for transfers between devices  9.48 us (7%)
  local copies, waits for them, and re-layouts  5.96 us (5%)
  other arithmetic  1.83 us (1%)
    dot_general x1, matrix products, shards(): jnp.einsum('imc,mn->icn', spectra_rows, dft_table, preferred_element_type...  70 us
    all_gather x1, blocking collectives, shards(): lax.all_gather(masked, 'lat', axis=1, tiled=True)  27.2 us
    all_to_all x1, starting transfers between devices, shards(): lax.all_to_all(by_dest, 'wave', split_axis=0, concat_axis=2, tiled=True)  11.9 us
    all_to_all x1, waiting for transfers between devices, shards(): lax.all_to_all(by_dest, 'wave', split_axis=0, concat_axis=2, tiled=True)  9.48 us
    gather x1, local copies, waits for them, and re-layouts, build_table(): frequency = MTOP - all_rows + 1 + assignment[table_row // 2]  5.01 us
  transfers between devices with their start and end apart: 1, of which 1 were waited for; matrix products, arithmetic and copies ran while one was open for 4% of the time, Pallas kernels for 0%

commit v1 on v0

v1 whole, which is shorter than its diff:
```python
import jax
import jax.numpy as jnp
from jax import lax
from jax.experimental import pallas as pl
from jax.experimental.pallas import tpu as pltpu
from jax.sharding import PartitionSpec as P

MTOP = 2559
C = 64
LONGITUDES = 5120
QUARTER = LONGITUDES // 4
LANES = 128
CHUNK = 256


def cos_sin_of_index(index):
    turn = jnp.floor((index + 0.5 * QUARTER) * (1.0 / QUARTER))
    rest = index - turn * QUARTER
    t = rest * (2.0 * 3.141592653589793 / LONGITUDES)
    t2 = t * t
    sin = t + t * t2 * (-1.6666667e-1 + t2 * (8.3333310e-3 + t2 * (-1.9840874e-4 + t2 * 2.7525562e-6)))
    cos = 1.0 + t2 * (-0.5 + t2 * (4.16666418e-2 + t2 * (-1.38888434e-3 + t2 * 2.47609e-5)))
    quadrant = turn - 4.0 * jnp.floor(turn * 0.25)
    odd = (quadrant == 1.0) | (quadrant == 3.0)
    cos_out = jnp.where(odd, sin, cos)
    sin_out = jnp.where(odd, cos, sin)
    cos_out = jnp.where((quadrant == 1.0) | (quadrant == 2.0), -cos_out, cos_out)
    sin_out = jnp.where(quadrant >= 2.0, -sin_out, sin_out)
    return cos_out, sin_out


def table_kernel(first, assignment_ref, table_ref):
    rows = assignment_ref.shape[1]
    slab = jnp.broadcast_to(assignment_ref[...], (LANES, rows)).astype(jnp.float32).T
    frequency = slab + float(first)
    lane = lax.broadcasted_iota(jnp.int32, (rows, LANES), 1).astype(jnp.float32)
    cos, sin = cos_sin_of_index(frequency * lane)
    step_cos, step_sin = cos_sin_of_index(frequency * float(LANES))
    cos, sin = 2.0 * cos, -2.0 * sin
    for block in range(QUARTER // LANES):
        columns = slice(block * LANES, (block + 1) * LANES)
        table_ref[:rows, columns] = cos.astype(table_ref.dtype)
        table_ref[rows:, columns] = sin.astype(table_ref.dtype)
        if block + 1 < QUARTER // LANES:
            cos, sin = cos * step_cos + sin * step_sin, sin * step_cos - cos * step_sin


def build_table(assignment):
    rows = assignment.shape[0]
    return pl.pallas_call(
        lambda a, t: table_kernel(MTOP - rows + 1, a, t),
        out_shape=jax.ShapeDtypeStruct((2 * rows, QUARTER), jnp.bfloat16),
        cost_estimate=pl.CostEstimate(flops=2 * 10 ** 9, bytes_accessed=2 * rows * QUARTER * 2, transcendentals=0),
        compiler_params=pltpu.CompilerParams(vmem_limit_bytes=16 * 2 ** 20),
        name="dft_table",
    )(assignment.reshape(1, rows))


def synthesis_kernel(first, assignment_ref, spectra_ref, table_ref, out_ref, lhs, buffer, semaphore):
    rows = assignment_ref.shape[1]
    items = spectra_ref.shape[0]
    quarter_turns = jnp.broadcast_to(assignment_ref[...], (LANES, rows)).T + first
    low = [spectra_ref[i].reshape(rows, 2 * C).astype(jnp.float32) for i in range(items)]
    real = jnp.concatenate([x[:, :C] for x in low], axis=1)
    imag = jnp.concatenate([x[:, C:] for x in low], axis=1)
    width = items * C
    for q in range(4):
        kind = (quarter_turns * q) % 4
        keep = jnp.where(kind == 0, 1.0, jnp.where(kind == 2, -1.0, 0.0)).astype(jnp.float32)
        swap = jnp.where(kind == 3, 1.0, jnp.where(kind == 1, -1.0, 0.0)).astype(jnp.float32)
        columns = slice(q * width, (q + 1) * width)
        lhs[:rows, columns] = (keep * real + swap * imag).astype(lhs.dtype)
        lhs[rows:, columns] = (keep * imag - swap * real).astype(lhs.dtype)
    chunks = QUARTER // CHUNK

    def copy(n, q):
        return pltpu.make_async_copy(
            buffer.at[n, q],
            out_ref.at[0, :, :, pl.ds(q * QUARTER + n * CHUNK, CHUNK)],
            semaphore.at[n, q],
        )

    for n in range(chunks):
        result = lax.dot_general(
            lhs[...], table_ref[:, n * CHUNK:(n + 1) * CHUNK],
            (((0,), (0,)), ((), ())), preferred_element_type=jnp.float32,
        )
        buffer[n] = result.reshape(4, items, C, CHUNK)
        for q in range(4):
            copy(n, q).start()
    for n in range(chunks):
        for q in range(4):
            copy(n, q).wait()


def synthesis(assignment, spectra, table):
    rows = assignment.shape[0]
    items = spectra.shape[0]
    chunks = QUARTER // CHUNK
    return pl.pallas_call(
        lambda *refs: synthesis_kernel(MTOP - rows + 1, *refs),
        out_shape=jax.ShapeDtypeStruct((1, items, C, LONGITUDES), jnp.float32),
        in_specs=[pl.BlockSpec(memory_space=pltpu.VMEM)] * 3,
        out_specs=pl.BlockSpec(memory_space=pl.ANY),
        scratch_shapes=[
            pltpu.VMEM((2 * rows, 4 * items * C), jnp.bfloat16),
            pltpu.VMEM((chunks, 4, items, C, CHUNK), jnp.float32),
            pltpu.SemaphoreType.DMA((chunks, 4)),
        ],
        cost_estimate=pl.CostEstimate(flops=10 ** 9, bytes_accessed=6 * 10 ** 6, transcendentals=0),
        compiler_params=pltpu.CompilerParams(vmem_limit_bytes=24 * 2 ** 20),
        name="synthesis",
    )(assignment.reshape(1, rows), spectra, table)


def shards(legendre, coefficients, assignment):
    row_count = legendre.shape[0]
    lat_count = legendre.shape[2]
    deg_count = coefficients.shape[1]
    all_rows = assignment.shape[0]
    wave_count = lax.axis_size("wave")
    lat_rows = lat_count // wave_count
    wave_index = lax.axis_index("wave")
    lat_index = lax.axis_index("lat")
    own_waves = lax.dynamic_slice_in_dim(assignment, wave_index * row_count, row_count)
    degree = lat_index * deg_count + jnp.arange(deg_count, dtype=jnp.int32)
    keep_mask = degree[None, :] < (all_rows - own_waves)[:, None]
    masked = jnp.where(keep_mask[:, :, None], coefficients, jnp.zeros_like(coefficients))
    lat_sum = jnp.einsum(
        "rkl,rkc->lrc",
        legendre,
        lax.all_gather(masked, "lat", axis=1, tiled=True),
        preferred_element_type=jnp.float32,
    )
    fields = lat_sum.astype(jnp.bfloat16)
    table = build_table(assignment)
    by_dest = fields.reshape(wave_count, lat_rows, row_count, fields.shape[2])
    exchanged = lax.all_to_all(by_dest, "wave", split_axis=0, concat_axis=2, tiled=True)
    spectra = exchanged.reshape(exchanged.shape[1], all_rows, 2 * C)
    return synthesis(assignment, spectra, table)


def solution(mesh):
    in_specs = (P("wave", None, "lat"), P("wave", "lat", None), P())
    out_specs = P("lat", "wave", None, None)
    return jax.shard_map(shards, mesh=mesh, in_specs=in_specs, out_specs=out_specs, check_vma=False)
```

time: 127 us -> 59.9 us (0.47)
  matrix products: 70.4 us -> 0.33 us
  local copies, waits for them, and re-layouts: 5.96 us -> 0.78 us
  Pallas kernels: 0 us -> 4.91 us
  waiting for transfers between devices: 9.48 us -> 12.7 us
    dot_general x1 -> x0, matrix products: 70 us -> none  [shards(): jnp.einsum('imc,mn->icn', spectra_rows, dft_table, preferred_element_type...]
    gather x1 -> x0, local copies, waits for them, and re-layouts: 5.01 us -> none  [build_table(): frequency = MTOP - all_rows + 1 + assignment[table_row // 2]]
    pallas_call x0 -> x2, Pallas kernels: none -> 4.91 us  [the longest x1 3.07 us: synthesis(): pl.pallas_call(lambda *refs: synthesis_kernel(MTOP - rows + 1, *refs), ou...]
    all_to_all x1, waiting for transfers between devices: 9.48 us -> 12.7 us  [shards(): lax.all_to_all(by_dest, 'wave', split_axis=0, concat_axis=2, tiled=True)]
  transfers between devices with their start and end apart: 1 -> 1, of which waited for: 1 -> 1; matrix products, arithmetic and copies ran while one was open for 4% -> 0% of each run, Pallas kernels for 0% -> 3%
where the time goes in v1:
time: 59.9 us; the launch traced here: 59.7 us
  blocking collectives  27.2 us (45%)
  waiting for transfers between devices  12.7 us (21%)
  starting transfers between devices  11.9 us (20%)
  Pallas kernels  4.91 us (8%)
  other arithmetic  1.79 us (3%)
  local copies, waits for them, and re-layouts  0.78 us (1%)
    all_gather x1, blocking collectives, shards(): lax.all_gather(masked, 'lat', axis=1, tiled=True)  27.2 us
    all_to_all x1, waiting for transfers between devices, shards(): lax.all_to_all(by_dest, 'wave', split_axis=0, concat_axis=2, tiled=True)  12.7 us
    all_to_all x1, starting transfers between devices, shards(): lax.all_to_all(by_dest, 'wave', split_axis=0, concat_axis=2, tiled=True)  11.9 us
    pallas_call x1, Pallas kernels, synthesis(): pl.pallas_call(lambda *refs: synthesis_kernel(MTOP - rows + 1, *refs), ou...  3.07 us
    pallas_call x1, Pallas kernels, build_table(): pl.pallas_call(lambda a, t: table_kernel(MTOP - rows + 1, a, t), out_shap...  1.84 us
  transfers between devices with their start and end apart: 1, of which 1 were waited for; matrix products, arithmetic and copies ran while one was open for 0% of the time, Pallas kernels for 3%

profile of v1, /device:TPU:1, one launch (start us, length us, event | category | flops | bytes accessed | tf_op | source)
XLA Modules:
  0.0 59.7 jit_solution(6195682515646455386)
XLA Ops:
  0.0 0.0 copy-start
  0.0 0.0 copy-start.1
  0.0 0.8 %dynamic-slice_subtract_fusion = s32[8]{0:T(128)S(1)} fusion(s32[384]{0:T(512)} %param.5, s32[]{:T(128)S(6)} %select_n.7), kind=kLoop, calls=%fused_computation.4 | loop fusion | flops 8 | bytes 68 | tf_op jit(solution)/shard_map/sub | solution.py:127
  0.8 0.1 broadcast_compare_fusion
  0.9 0.9 %broadcast_select_fusion = bf16[8,24,128]{2,1,0:T(8,128)(2,1)S(1)} fusion(bf16[8,24,128]{2,1,0:T(8,128)(2,1)} %param.4, pred[8,24]{1,0:T(8,128)(4,1)S(1)} %broadcast_compare_fusion), kind=kLoop, calls=%fused_computation.2 | loop fusion | flops 24576 | bytes 98496 | tf_op jit(solution)/shard_map/jit(_where)/select_n | solution.py:128
  1.8 27.2 %all_gather.3 = bf16[8,384,128]{2,1,0:T(8,128)(2,1)S(1)} all-gather(bf16[8,24,128]{2,1,0:T(8,128)(2,1)S(1)} %broadcast_select_fusion), channel_id=1, replica_groups=mesh['wave'=48,'lat'=16] {'lat'}, dimensions={1}, use_global_device_ids=true | all-gather | bytes 835584 | tf_op jit(solution)/shard_map/all_gather | solution.py:132
  29.0 0.0 copy-done
  29.0 0.3 convolution_convert_fusion
  29.3 0.8 %copy.5 = bf16[48,2,8,128]{3,2,1,0:T(8,128)(2,1)} copy(bf16[48,2,8,128]{3,1,0,2:T(2,128)(2,1)S(1)} %bitcast.12) | data formatting | bytes 393216 | tf_op jit(solution)/shard_map/reshape | solution.py:137
  30.1 11.9 %all-to-all-start = ((bf16[48,2,8,128]{3,2,1,0:T(8,128)(2,1)}), bf16[48,2,8,128]{3,2,1,0:T(8,128)(2,1)S(1)}, u32[]{:S(2)}, u32[]{:S(2)}) async-start(bf16[48,2,8,128]{3,2,1,0:T(8,128)(2,1)} %copy.5), calls=%async_computation | async-start | bytes 393216 | tf_op jit(solution)/shard_map/all_to_all | solution.py:138
  42.0 0.0 copy-done.1
  42.0 1.8 %dft_table.1.refs_2_ = bf16[768,1280]{1,0:T(8,128)(2,1)S(1)} custom-call(s32[1,384]{1,0:T(1,128)S(1)} %reshape.43.a.refs_0_), custom_call_target="tpu_custom_call" | custom-call | flops 2000000000 | bytes 1966080 | tf_op jit(solution)/shard_map/dft_table/pallas_call | solution.py:50
  43.9 12.7 %all-to-all-done = bf16[48,2,8,128]{3,2,1,0:T(8,128)(2,1)S(1)} async-done(((bf16[48,2,8,128]{3,2,1,0:T(8,128)(2,1)}), bf16[48,2,8,128]{3,2,1,0:T(8,128)(2,1)S(1)}, u32[]{:S(2)}, u32[]{:S(2)}) %all-to-all-start) | async-done | bytes 196640 | tf_op jit(solution)/shard_map/all_to_all | solution.py:138
  56.6 3.1 %synthesis.1 = f32[1,2,64,5120]{3,2,1,0:T(8,128)} custom-call(s32[1,384]{1,0:T(1,128)S(1)} %reshape.43.a.refs_0_, bf16[2,384,128]{2,1,0:T(8,128)(2,1)S(1)} %copy_bitcast_fusion.refs_1_, bf16[768,1280]{1,0:T(8,128)(2,1)S(1)} %dft_table.1.refs_2_), custom_call_target="tpu_custom_call" | custom-call | flops 1000000000 | bytes 6000000 | tf_op jit(solution)/shard_map/synthesis/pallas_call | solution.py:100
  (3 shorter events, 0.0 us)
Async XLA Ops:
  0.0 29.0 %copy-start = (bf16[8,384,96]{1,2,0:T(8,128)(2,1)S(1)}, bf16[8,384,96]{1,2,0:T(8,128)(2,1)}, u32[]{:S(2)}) copy-start(bf16[8,384,96]{1,2,0:T(8,128)(2,1)} %param.3) | copy-start | bytes 1769476
  0.0 42.0 %copy-start.1 = (s32[384]{0:T(512)S(1)}, s32[384]{0:T(512)}, u32[]{:S(2)}) copy-start(s32[384]{0:T(512)} %param.5) | copy-start | bytes 4612
  30.1 26.5 %all-to-all-start = ((bf16[48,2,8,128]{3,2,1,0:T(8,128)(2,1)}), bf16[48,2,8,128]{3,2,1,0:T(8,128)(2,1)S(1)}, u32[]{:S(2)}, u32[]{:S(2)}) async-start(bf16[48,2,8,128]{3,2,1,0:T(8,128)(2,1)} %copy.5), calls=%async_computation | async-start | bytes 393216 | tf_op jit(solution)/shard_map/all_to_all | solution.py:138

commit v2 on v1

v2 whole, which is shorter than its diff:
```python
import jax
import jax.numpy as jnp
from jax import lax
from jax.experimental import pallas as pl
from jax.experimental.pallas import tpu as pltpu
from jax.sharding import PartitionSpec as P

MTOP = 2559
C = 64
LONGITUDES = 5120
QUARTER = LONGITUDES // 4
LANES = 128
CHUNK = 256
BLOCK_OF_CLASS = (0, 2, 1, 3)


def cos_sin_of_index(index):
    turn = jnp.floor((index + 0.5 * QUARTER) * (1.0 / QUARTER))
    rest = index - turn * QUARTER
    t = rest * (2.0 * 3.141592653589793 / LONGITUDES)
    t2 = t * t
    sin = t + t * t2 * (-1.6666667e-1 + t2 * (8.3333310e-3 + t2 * (-1.9840874e-4 + t2 * 2.7525562e-6)))
    cos = 1.0 + t2 * (-0.5 + t2 * (4.16666418e-2 + t2 * (-1.38888434e-3 + t2 * 2.47609e-5)))
    quadrant = turn - 4.0 * jnp.floor(turn * 0.25)
    odd = (quadrant == 1.0) | (quadrant == 3.0)
    cos_out = jnp.where(odd, sin, cos)
    sin_out = jnp.where(odd, cos, sin)
    cos_out = jnp.where((quadrant == 1.0) | (quadrant == 2.0), -cos_out, cos_out)
    sin_out = jnp.where(quadrant >= 2.0, -sin_out, sin_out)
    return cos_out, sin_out


def fields_kernel(assignment_ref, legendre_ref, coefficients_ref, out_ref):
    row_count, lat_count, deg_count = legendre_ref.shape
    all_rows = assignment_ref.shape[0]
    first_row = lax.axis_index("wave") * row_count
    degree = lax.broadcasted_iota(jnp.int32, (1, deg_count), 1)
    sums = []
    for row in range(row_count):
        kept = all_rows - assignment_ref[first_row + row]
        mask = jnp.where(degree < kept, 1.0, 0.0).astype(jnp.bfloat16)
        sums.append(jnp.dot(legendre_ref[row] * mask, coefficients_ref[row], preferred_element_type=jnp.float32))
    out = jnp.stack(sums, axis=1)
    out_ref[...] = out.reshape(out_ref.shape).astype(out_ref.dtype)


def legendre_sums(assignment, legendre, coefficients, wave_count):
    row_count, lat_count, deg_count = legendre.shape
    columns = coefficients.shape[2]
    return pl.pallas_call(
        fields_kernel,
        out_shape=jax.ShapeDtypeStruct((wave_count, lat_count // wave_count, row_count, columns), jnp.bfloat16),
        in_specs=[
            pl.BlockSpec(memory_space=pltpu.SMEM),
            pl.BlockSpec(memory_space=pltpu.VMEM),
            pl.BlockSpec(memory_space=pltpu.VMEM),
        ],
        out_specs=pl.BlockSpec(memory_space=pltpu.VMEM),
        compiler_params=pltpu.CompilerParams(vmem_limit_bytes=16 * 2 ** 20),
        name="legendre_sums",
    )(assignment, legendre, coefficients)


def tables_kernel(first, row_count, items, assignment_ref, table_ref, place_ref):
    rows = assignment_ref.shape[1]
    classes = len(BLOCK_OF_CLASS)
    padded = classes * LANES
    slab = jnp.broadcast_to(assignment_ref[...], (LANES, rows)).T
    kind = slab % classes
    block = jnp.where(kind == 1, 2, jnp.where(kind == 2, 1, kind))
    target = block * LANES + slab // classes
    lane = lax.broadcasted_iota(jnp.int32, (rows // row_count, items, row_count, LANES), 3)
    item = lax.broadcasted_iota(jnp.int32, (rows // row_count, items, row_count, LANES), 1)
    target = target.reshape(rows // row_count, 1, row_count, LANES) + item * padded - lane
    target = target.reshape(items * rows, LANES)
    for n in range(items * classes):
        place_ref[:, n * LANES:(n + 1) * LANES] = jnp.where(target == n * LANES, 1.0, 0.0).astype(place_ref.dtype)

    lane = lax.broadcasted_iota(jnp.int32, (LANES, LANES), 1).astype(jnp.float32)
    count = lax.broadcasted_iota(jnp.int32, (LANES, LANES), 0).astype(jnp.float32)
    for cls, position in enumerate(BLOCK_OF_CLASS):
        frequency = float(first + cls) + classes * count
        cos, sin = cos_sin_of_index(frequency * lane)
        step_cos, step_sin = cos_sin_of_index(frequency * float(LANES))
        cos, sin = 2.0 * cos, -2.0 * sin
        half, slot = divmod(position, 2)
        cos_rows = slice((4 * half + slot) * LANES, (4 * half + slot + 1) * LANES)
        sin_rows = slice((4 * half + slot + 2) * LANES, (4 * half + slot + 3) * LANES)
        for column in range(QUARTER // LANES):
            columns = slice(column * LANES, (column + 1) * LANES)
            table_ref[cos_rows, columns] = cos.astype(table_ref.dtype)
            table_ref[sin_rows, columns] = sin.astype(table_ref.dtype)
            if column + 1 < QUARTER // LANES:
                cos, sin = cos * step_cos + sin * step_sin, sin * step_cos - cos * step_sin


def build_tables(assignment, row_count, items):
    rows = assignment.shape[0]
    padded = len(BLOCK_OF_CLASS) * LANES
    return pl.pallas_call(
        lambda *refs: tables_kernel(MTOP - rows + 1, row_count, items, *refs),
        out_shape=(
            jax.ShapeDtypeStruct((2 * padded, QUARTER), jnp.bfloat16),
            jax.ShapeDtypeStruct((items * rows, items * padded), jnp.bfloat16),
        ),
        in_specs=[pl.BlockSpec(memory_space=pltpu.VMEM)],
        out_specs=(pl.BlockSpec(memory_space=pltpu.VMEM), pl.BlockSpec(memory_space=pltpu.VMEM)),
        cost_estimate=pl.CostEstimate(flops=2 * 10 ** 9, bytes_accessed=5 * 10 ** 6, transcendentals=0),
        compiler_params=pltpu.CompilerParams(vmem_limit_bytes=20 * 2 ** 20),
        name="dft_tables",
    )(assignment.reshape(1, rows))


def synthesis_kernel(items, spectra_ref, place_ref, table_ref, out_ref, buffer, semaphore):
    padded = len(BLOCK_OF_CLASS) * LANES
    placed = lax.dot_general(
        spectra_ref[...], place_ref[...], (((0,), (0,)), ((), ())), preferred_element_type=jnp.float32
    ).astype(jnp.bfloat16)

    def part(half, item, block):
        return placed[half * C:(half + 1) * C, item * padded + block * LANES:item * padded + (block + 1) * LANES]

    def rows_of(blocks):
        return jnp.concatenate([jnp.concatenate([f(i) for f in blocks], axis=1) for i in range(items)], axis=0)

    even = jnp.concatenate([
        rows_of([lambda i: part(0, i, 0), lambda i: part(0, i, 1), lambda i: part(1, i, 0), lambda i: part(1, i, 1)]),
        rows_of([lambda i: part(0, i, 0), lambda i: -part(0, i, 1), lambda i: part(1, i, 0), lambda i: -part(1, i, 1)]),
    ], axis=0)
    odd = jnp.concatenate([
        rows_of([lambda i: part(0, i, 2), lambda i: part(0, i, 3), lambda i: part(1, i, 2), lambda i: part(1, i, 3)]),
        rows_of([lambda i: -part(1, i, 2), lambda i: part(1, i, 3), lambda i: part(0, i, 2), lambda i: -part(0, i, 3)]),
    ], axis=0)
    chunks = QUARTER // CHUNK

    def copy(n, q):
        return pltpu.make_async_copy(
            buffer.at[n, q],
            out_ref.at[0, :, :, pl.ds(q * QUARTER + n * CHUNK, CHUNK)],
            semaphore.at[n, q],
        )

    for n in range(chunks):
        columns = slice(n * CHUNK, (n + 1) * CHUNK)
        from_even = jnp.dot(even, table_ref[:padded, columns], preferred_element_type=jnp.float32)
        from_odd = jnp.dot(odd, table_ref[padded:, columns], preferred_element_type=jnp.float32)
        buffer[n, :2] = (from_even + from_odd).reshape(2, items, C, CHUNK)
        buffer[n, 2:] = (from_even - from_odd).reshape(2, items, C, CHUNK)
        for q in range(4):
            copy(n, q).start()
    for n in range(chunks):
        for q in range(4):
            copy(n, q).wait()


def synthesis(spectra, place, table, items):
    chunks = QUARTER // CHUNK
    return pl.pallas_call(
        lambda *refs: synthesis_kernel(items, *refs),
        out_shape=jax.ShapeDtypeStruct((1, items, C, LONGITUDES), jnp.float32),
        in_specs=[pl.BlockSpec(memory_space=pltpu.VMEM)] * 3,
        out_specs=pl.BlockSpec(memory_space=pl.ANY),
        scratch_shapes=[
            pltpu.VMEM((chunks, 4, items, C, CHUNK), jnp.float32),
            pltpu.SemaphoreType.DMA((chunks, 4)),
        ],
        cost_estimate=pl.CostEstimate(flops=10 ** 9, bytes_accessed=6 * 10 ** 6, transcendentals=0),
        compiler_params=pltpu.CompilerParams(vmem_limit_bytes=24 * 2 ** 20),
        name="synthesis",
    )(spectra, place, table)


def shards(legendre, coefficients, assignment):
    row_count = legendre.shape[0]
    all_rows = assignment.shape[0]
    wave_count = lax.axis_size("wave")
    items = legendre.shape[2] // wave_count
    gathered = lax.all_gather(coefficients, "lat", axis=1, tiled=True)
    by_dest = legendre_sums(assignment, jnp.swapaxes(legendre, 1, 2), gathered, wave_count)
    exchanged = lax.all_to_all(by_dest, "wave", split_axis=0, concat_axis=0, tiled=True)
    table, place = build_tables(assignment, row_count, items)
    return synthesis(exchanged.reshape(items * all_rows, 2 * C), place, table, items)


def solution(mesh):
    in_specs = (P("wave", None, "lat"), P("wave", "lat", None), P())
    out_specs = P("lat", "wave", None, None)
    return jax.shard_map(shards, mesh=mesh, in_specs=in_specs, out_specs=out_specs, check_vma=False)
```

time: 59.9 us -> 61.5 us (1.027)
  local copies, waits for them, and re-layouts: 0.78 us -> 4.3 us
  waiting for transfers between devices: 12.7 us -> 10.8 us
  other arithmetic: 1.79 us -> 0 us
  Pallas kernels: 4.91 us -> 6.67 us
    unnamed x4 -> x10, local copies, waits for them, and re-layouts: 0.01 us -> 4.29 us
    all_to_all x1, waiting for transfers between devices: 12.7 us -> 10.8 us  [shards(): lax.all_to_all(by_dest, 'wave', split_axis=0, concat_axis=0, tiled=True)]
    pallas_call x2 -> x3, Pallas kernels: 4.91 us -> 6.67 us  [the longest x1 2.61 us: build_tables(): pl.pallas_call(lambda *refs: tables_kernel(MTOP - rows + 1, row_count, it...]
    select_n x1 -> x0, other arithmetic: 0.89 us -> none  [shards(): jnp.where(keep_mask[:, :, None], coefficients, jnp.zeros_like(coefficients))]
    sub x1 -> x0, other arithmetic: 0.82 us -> none  [shards(): keep_mask = degree[None, :] < (all_rows - own_waves)[:, None]]
    reshape x3 -> x1, local copies, waits for them, and re-layouts: 0.77 us -> 0.01 us  [build_tables(): assignment.reshape(1, rows)]
  transfers between devices with their start and end apart: 1 -> 1, of which waited for: 1 -> 1; matrix products, arithmetic and copies ran while one was open for 0% -> 0% of each run, Pallas kernels for 3% -> 4%
where the time goes in v2:
time: 61.5 us; the launch traced here: 61.2 us
  blocking collectives  27.6 us (45%)
  starting transfers between devices  11.9 us (19%)
  waiting for transfers between devices  10.8 us (18%)
  Pallas kernels  6.67 us (11%)
  local copies, waits for them, and re-layouts  4.3 us (7%)
    all_gather x1, blocking collectives, shards(): gathered = lax.all_gather(coefficients, 'lat', axis=1, tiled=True)  27.6 us
    all_to_all x1, starting transfers between devices, shards(): lax.all_to_all(by_dest, 'wave', split_axis=0, concat_axis=0, tiled=True)  11.9 us
    all_to_all x1, waiting for transfers between devices, shards(): lax.all_to_all(by_dest, 'wave', split_axis=0, concat_axis=0, tiled=True)  10.8 us
    unnamed x10, local copies, waits for them, and re-layouts  4.29 us
    pallas_call x1, Pallas kernels, build_tables(): pl.pallas_call(lambda *refs: tables_kernel(MTOP - rows + 1, row_count, it...  2.61 us
    pallas_call x1, Pallas kernels, synthesis(): pl.pallas_call(lambda *refs: synthesis_kernel(items, *refs), out_shape=ja...  2.27 us
    pallas_call x1, Pallas kernels, legendre_sums(): pl.pallas_call(fields_kernel, out_shape=jax.ShapeDtypeStruct((wave_count,...  1.79 us
  transfers between devices with their start and end apart: 1, of which 1 were waited for; matrix products, arithmetic and copies ran while one was open for 0% of the time, Pallas kernels for 4%

profile of v2, /device:TPU:1, one launch (start us, length us, event | category | flops | bytes accessed | tf_op | source)
XLA Modules:
  0.0 61.2 jit_solution(3962397146587257664)
XLA Ops:
  0.0 0.0 copy-start.4
  0.0 27.6 %all_gather.3.coefficients_ref = bf16[8,384,128]{2,1,0:T(8,128)(2,1)S(1)} all-gather(bf16[8,24,128]{2,1,0:T(8,128)(2,1)} %param.4), channel_id=1, replica_groups=mesh['wave'=48,'lat'=16] {'lat'}, dimensions={1}, use_global_device_ids=true | all-gather | bytes 835584 | tf_op jit(solution)/shard_map/all_gather | solution.py:178
  27.6 0.0 copy-start.2
  27.6 1.1 %copy-done.2 = bf16[8,384,96]{1,2,0:T(8,128)(2,1)S(1)} copy-done((bf16[8,384,96]{1,2,0:T(8,128)(2,1)S(1)}, bf16[8,384,96]{1,2,0:T(8,128)(2,1)}, u32[]{:S(2)}) %copy-start.2) | copy-done | bytes 589848
  28.6 0.0 copy-start.3
  28.6 0.7 %copy-done.3 = s32[384]{0:T(512)S(1)} copy-done((s32[384]{0:T(512)S(1)}, s32[384]{0:T(512)}, u32[]{:S(2)}) %copy-start.3) | copy-done | bytes 1560
  29.3 1.8 %legendre_sums.1 = bf16[48,2,8,128]{3,2,1,0:T(8,128)(2,1)} custom-call(s32[384]{0:T(512)S(1)} %copy-done.3, bf16[8,96,384]{2,1,0:T(8,128)(2,1)S(1)} %bitcast.3, bf16[8,384,128]{2,1,0:T(8,128)(2,1)S(1)} %all_gather.3.coefficients_ref), custom_call_target="tpu_custom_call" | custom-call | tf_op jit(solution)/shard_map/legendre_sums/pallas_call | solution.py:50
  31.1 11.9 %all-to-all-start = ((bf16[48,2,8,128]{3,2,1,0:T(8,128)(2,1)}), bf16[48,2,8,128]{3,2,1,0:T(8,128)(2,1)S(1)}, u32[]{:S(2)}, u32[]{:S(2)}) async-start(bf16[48,2,8,128]{3,2,1,0:T(8,128)(2,1)} %legendre_sums.1), calls=%async_computation | async-start | bytes 393216 | tf_op jit(solution)/shard_map/all_to_all | solution.py:180
  43.0 0.0 copy-done.4
  43.0 2.6 %dft_tables.1 = (bf16[1024,1280]{1,0:T(8,128)(2,1)S(1)}, bf16[768,1024]{1,0:T(8,128)(2,1)S(1)}) custom-call(s32[1,384]{1,0:T(1,128)S(1)} %reshape.7.refs_0_), custom_call_target="tpu_custom_call" | custom-call | flops 2000000000 | bytes 5000000 | tf_op jit(solution)/shard_map/dft_tables/pallas_call | solution.py:100
  45.6 0.0 copy-start
  45.7 1.1 %copy-done = bf16[768,1024]{1,0:T(8,128)(2,1)} copy-done((bf16[768,1024]{1,0:T(8,128)(2,1)}, bf16[768,1024]{1,0:T(8,128)(2,1)S(1)}, u32[]{:S(2)}) %copy-start) | copy-done | bytes 1572888
  46.8 10.8 %all-to-all-done = bf16[48,2,8,128]{3,2,1,0:T(8,128)(2,1)S(1)} async-done(((bf16[48,2,8,128]{3,2,1,0:T(8,128)(2,1)}), bf16[48,2,8,128]{3,2,1,0:T(8,128)(2,1)S(1)}, u32[]{:S(2)}, u32[]{:S(2)}) %all-to-all-start) | async-done | bytes 196640 | tf_op jit(solution)/shard_map/all_to_all | solution.py:180
  57.6 0.0 copy-start.1
  57.6 1.4 %copy-done.1 = bf16[768,1024]{1,0:T(8,128)(2,1)S(1)} copy-done((bf16[768,1024]{1,0:T(8,128)(2,1)S(1)}, bf16[768,1024]{1,0:T(8,128)(2,1)}, u32[]{:S(2)}) %copy-start.1) | copy-done | bytes 1572888
  59.0 2.3 %synthesis.1 = f32[1,2,64,5120]{3,2,1,0:T(8,128)} custom-call(bf16[768,128]{1,0:T(8,128)(2,1)S(1)} %bitcast.2, bf16[768,1024]{1,0:T(8,128)(2,1)S(1)} %copy-done.1, bf16[1024,1280]{1,0:T(8,128)(2,1)S(1)} %get-tuple-element.8.refs_2_), custom_call_target="tpu_custom_call" | custom-call | flops 1000000000 | bytes 6000000 | tf_op jit(solution)/shard_map/synthesis/pallas_call | solution.py:158
  (1 shorter events, 0.0 us)
Async XLA Ops:
  0.0 43.0 %copy-start.4 = (s32[384]{0:T(512)S(1)}, s32[384]{0:T(512)}, u32[]{:S(2)}) copy-start(s32[384]{0:T(512)} %assignment_ref.1) | copy-start | bytes 4612
  27.6 1.1 %copy-start.2 = (bf16[8,384,96]{1,2,0:T(8,128)(2,1)S(1)}, bf16[8,384,96]{1,2,0:T(8,128)(2,1)}, u32[]{:S(2)}) copy-start(bf16[8,384,96]{1,2,0:T(8,128)(2,1)} %param.3) | copy-start | bytes 1769476
  28.6 0.7 %copy-start.3 = (s32[384]{0:T(512)S(1)}, s32[384]{0:T(512)}, u32[]{:S(2)}) copy-start(s32[384]{0:T(512)} %assignment_ref.1) | copy-start | bytes 4612
  31.1 26.5 %all-to-all-start = ((bf16[48,2,8,128]{3,2,1,0:T(8,128)(2,1)}), bf16[48,2,8,128]{3,2,1,0:T(8,128)(2,1)S(1)}, u32[]{:S(2)}, u32[]{:S(2)}) async-start(bf16[48,2,8,128]{3,2,1,0:T(8,128)(2,1)} %legendre_sums.1), calls=%async_computation | async-start | bytes 393216 | tf_op jit(solution)/shard_map/all_to_all | solution.py:180
  45.6 1.1 %copy-start = (bf16[768,1024]{1,0:T(8,128)(2,1)}, bf16[768,1024]{1,0:T(8,128)(2,1)S(1)}, u32[]{:S(2)}) copy-start(bf16[768,1024]{1,0:T(8,128)(2,1)S(1)} %get-tuple-element.7.refs_1_) | copy-start | bytes 4718596
  57.6 1.4 %copy-start.1 = (bf16[768,1024]{1,0:T(8,128)(2,1)S(1)}, bf16[768,1024]{1,0:T(8,128)(2,1)}, u32[]{:S(2)}) copy-start(bf16[768,1024]{1,0:T(8,128)(2,1)} %copy-done) | copy-start | bytes 4718596

commit v3 on v0

v3 whole, which is shorter than its diff:
```python
import jax
import jax.numpy as jnp
import numpy as np
from jax import lax
from jax.experimental import pallas as pl
from jax.experimental.pallas import tpu as pltpu
from jax.sharding import PartitionSpec as P

MTOP = 2559
C = 64
LONGITUDES = 5120
QUARTER = LONGITUDES // 4
LANES = 128
CHUNK = 256
BLOCK_OF_CLASS = (0, 2, 1, 3)


def synthesis_table(first, rows):
    classes = len(BLOCK_OF_CLASS)
    table = np.zeros((2 * classes, LANES, QUARTER), np.float32)
    for cls, position in enumerate(BLOCK_OF_CLASS):
        frequency = first + np.arange(cls, rows, classes)
        phase = (frequency[:, None] * np.arange(QUARTER)[None, :]) % LONGITUDES
        angle = phase * (2.0 * np.pi / LONGITUDES)
        half, slot = divmod(position, 2)
        table[4 * half + slot, :len(frequency)] = 2.0 * np.cos(angle)
        table[4 * half + slot + 2, :len(frequency)] = -2.0 * np.sin(angle)
    return jnp.asarray(table.reshape(-1, QUARTER).astype(jnp.bfloat16))


def degrees_kernel(out_ref):
    out_ref[...] = lax.broadcasted_iota(jnp.int32, out_ref.shape, 1)


def degree_row(count):
    return pl.pallas_call(
        degrees_kernel,
        out_shape=jax.ShapeDtypeStruct((1, count), jnp.int32),
        out_specs=pl.BlockSpec(memory_space=pltpu.VMEM),
        cost_estimate=pl.CostEstimate(flops=10 ** 9, bytes_accessed=4 * count, transcendentals=0),
        compiler_params=pltpu.CompilerParams(vmem_limit_bytes=2 ** 20),
        name="degree_row",
    )()


def fields_kernel(assignment_ref, degree_ref, legendre_ref, coefficients_ref, out_ref, place_ref, by_latitude):
    row_count, lat_count, deg_count = legendre_ref.shape
    all_rows = assignment_ref.shape[1]
    first_row = lax.axis_index("wave") * row_count
    place = lax.broadcasted_iota(jnp.int32, (1, all_rows), 1)
    degree = degree_ref[...]
    slab = assignment_ref[...]
    for row in range(row_count):
        own = jnp.sum(jnp.where(place == first_row + row, slab, 0), axis=1, keepdims=True)
        mask = jnp.where(degree < all_rows - own, 1.0, 0.0).astype(jnp.bfloat16)
        by_latitude[pl.ds(row, lat_count, stride=row_count), :] = jnp.dot(
            legendre_ref[row] * mask, coefficients_ref[row], preferred_element_type=jnp.float32
        )
    out_ref[...] = by_latitude[...].astype(out_ref.dtype).reshape(out_ref.shape)
    classes = len(BLOCK_OF_CLASS)
    slab = jnp.broadcast_to(slab, (LANES, all_rows)).T
    kind = slab % classes
    block = jnp.where(kind == 1, 2, jnp.where(kind == 2, 1, kind))
    target = block * LANES + slab // classes - lax.broadcasted_iota(jnp.int32, slab.shape, 1)
    for n in range(classes):
        place_ref[:, n * LANES:(n + 1) * LANES] = jnp.where(target == n * LANES, 1.0, 0.0).astype(place_ref.dtype)


def legendre_sums(assignment, degree, legendre, coefficients, wave_count):
    row_count, lat_count, deg_count = legendre.shape
    columns = coefficients.shape[2]
    return pl.pallas_call(
        fields_kernel,
        out_shape=(
            jax.ShapeDtypeStruct((wave_count, lat_count // wave_count, row_count, columns), jnp.bfloat16),
            jax.ShapeDtypeStruct((assignment.shape[0], len(BLOCK_OF_CLASS) * LANES), jnp.bfloat16),
        ),
        in_specs=[pl.BlockSpec(memory_space=pltpu.VMEM)] * 4,
        out_specs=(pl.BlockSpec(memory_space=pltpu.VMEM), pl.BlockSpec(memory_space=pltpu.VMEM)),
        scratch_shapes=[pltpu.VMEM((row_count * lat_count, columns), jnp.float32)],
        compiler_params=pltpu.CompilerParams(vmem_limit_bytes=16 * 2 ** 20),
        name="legendre_sums",
    )(assignment.reshape(1, -1), degree, legendre, coefficients)


def synthesis_kernel(spectra_ref, place_ref, table_ref, out_ref, buffer, semaphore):
    items = spectra_ref.shape[1]
    rows, padded = place_ref.shape
    placed = []
    for i in range(items):
        spectra = spectra_ref[:, i].astype(jnp.float32).reshape(rows, 2 * C).astype(jnp.bfloat16)
        placed.append(lax.dot_general(
            spectra, place_ref[...], (((0,), (0,)), ((), ())), preferred_element_type=jnp.float32
        ).astype(jnp.bfloat16))

    def part(half, item, block):
        return placed[item][half * C:(half + 1) * C, block * LANES:(block + 1) * LANES]

    def rows_of(blocks):
        return jnp.concatenate([jnp.concatenate([f(i) for f in blocks], axis=1) for i in range(items)], axis=0)

    even = jnp.concatenate([
        rows_of([lambda i: part(0, i, 0), lambda i: part(0, i, 1), lambda i: part(1, i, 0), lambda i: part(1, i, 1)]),
        rows_of([lambda i: part(0, i, 0), lambda i: -part(0, i, 1), lambda i: part(1, i, 0), lambda i: -part(1, i, 1)]),
    ], axis=0)
    odd = jnp.concatenate([
        rows_of([lambda i: part(0, i, 2), lambda i: part(0, i, 3), lambda i: part(1, i, 2), lambda i: part(1, i, 3)]),
        rows_of([lambda i: -part(1, i, 2), lambda i: part(1, i, 3), lambda i: part(0, i, 2), lambda i: -part(0, i, 3)]),
    ], axis=0)
    chunks = QUARTER // CHUNK

    def copy(n, q):
        return pltpu.make_async_copy(
            buffer.at[n, q],
            out_ref.at[0, :, :, pl.ds(q * QUARTER + n * CHUNK, CHUNK)],
            semaphore.at[n, q],
        )

    for n in range(chunks):
        columns = slice(n * CHUNK, (n + 1) * CHUNK)
        from_even = jnp.dot(even, table_ref[:padded, columns], preferred_element_type=jnp.float32)
        from_odd = jnp.dot(odd, table_ref[padded:, columns], preferred_element_type=jnp.float32)
        buffer[n, :2] = (from_even + from_odd).reshape(2, items, C, CHUNK)
        buffer[n, 2:] = (from_even - from_odd).reshape(2, items, C, CHUNK)
        for q in range(4):
            copy(n, q).start()
    for n in range(chunks):
        for q in range(4):
            copy(n, q).wait()


def synthesis(spectra, place, table):
    items = spectra.shape[1]
    chunks = QUARTER // CHUNK
    return pl.pallas_call(
        synthesis_kernel,
        out_shape=jax.ShapeDtypeStruct((1, items, C, LONGITUDES), jnp.float32),
        in_specs=[pl.BlockSpec(memory_space=pltpu.VMEM)] * 3,
        out_specs=pl.BlockSpec(memory_space=pl.ANY),
        scratch_shapes=[
            pltpu.VMEM((chunks, 4, items, C, CHUNK), jnp.float32),
            pltpu.SemaphoreType.DMA((chunks, 4)),
        ],
        cost_estimate=pl.CostEstimate(flops=10 ** 9, bytes_accessed=6 * 10 ** 6, transcendentals=0),
        compiler_params=pltpu.CompilerParams(vmem_limit_bytes=24 * 2 ** 20),
        name="synthesis",
    )(spectra, place, table)


def shards(legendre, coefficients, assignment):
    wave_count = lax.axis_size("wave")
    coefficients, degree = lax.optimization_barrier((coefficients, degree_row(legendre.shape[1])))
    gathered = lax.all_gather(coefficients, "lat", axis=1, tiled=True)
    gathered, assignment = lax.optimization_barrier((gathered, assignment))
    by_dest, place = legendre_sums(assignment, degree, jnp.swapaxes(legendre, 1, 2), gathered, wave_count)
    exchanged = lax.all_to_all(by_dest, "wave", split_axis=0, concat_axis=0, tiled=True)
    table = synthesis_table(MTOP - assignment.shape[0] + 1, assignment.shape[0])
    return synthesis(exchanged, place, table)


def solution(mesh):
    in_specs = (P("wave", None, "lat"), P("wave", "lat", None), P())
    out_specs = P("lat", "wave", None, None)
    return jax.shard_map(shards, mesh=mesh, in_specs=in_specs, out_specs=out_specs, check_vma=False)
```

time: 127 us -> 57.5 us (0.45)
  matrix products: 70.4 us -> 0 us
  blocking collectives: 27.2 us -> 53.6 us
  starting transfers between devices: 11.9 us -> 0 us
  waiting for transfers between devices: 9.48 us -> 0 us
  local copies, waits for them, and re-layouts: 5.96 us -> 0.93 us
  Pallas kernels: 0 us -> 2.78 us
  other arithmetic: 1.83 us -> 0 us
    dot_general x2 -> x0, matrix products: 70.4 us -> none  [the longest x1 70 us: shards(): jnp.einsum('imc,mn->icn', spectra_rows, dft_table, preferred_element_type...]
    all_to_all x0 -> x1, blocking collectives: none -> 26.3 us  [shards(): lax.all_to_all(by_dest, 'wave', split_axis=0, concat_axis=0, tiled=True)]
    all_to_all x1 -> x0, starting transfers between devices: 11.9 us -> none  [shards(): lax.all_to_all(by_dest, 'wave', split_axis=0, concat_axis=2, tiled=True)]
    all_to_all x1 -> x0, waiting for transfers between devices: 9.48 us -> none  [shards(): lax.all_to_all(by_dest, 'wave', split_axis=0, concat_axis=2, tiled=True)]
    gather x1 -> x0, local copies, waits for them, and re-layouts: 5.01 us -> none  [build_table(): frequency = MTOP - all_rows + 1 + assignment[table_row // 2]]
    pallas_call x0 -> x3, Pallas kernels: none -> 2.78 us  [the longest x1 2.18 us: synthesis(): pl.pallas_call(synthesis_kernel, out_shape=jax.ShapeDtypeStruct((1, items...]
  transfers between devices with their start and end apart: 1 -> 0, of which waited for: 1 -> 0; matrix products, arithmetic and copies ran while one was open for 4% -> 0% of each run, Pallas kernels for 0% -> 0%
where the time goes in v3:
time: 57.5 us; the launch traced here: 57.3 us
  blocking collectives  53.6 us (93%)
  Pallas kernels  2.78 us (5%)
  local copies, waits for them, and re-layouts  0.93 us (2%)
    all_gather x1, blocking collectives, shards(): gathered = lax.all_gather(coefficients, 'lat', axis=1, tiled=True)  27.3 us
    all_to_all x1, blocking collectives, shards(): lax.all_to_all(by_dest, 'wave', split_axis=0, concat_axis=0, tiled=True)  26.3 us
    pallas_call x1, Pallas kernels, synthesis(): pl.pallas_call(synthesis_kernel, out_shape=jax.ShapeDtypeStruct((1, items...  2.18 us

profile of v3, /device:TPU:1, one launch (start us, length us, event | category | flops | bytes accessed | tf_op | source)
XLA Modules:
  0.0 57.3 jit_solution(10213682024677226839)
XLA Ops:
  0.0 0.0 copy-start
  0.0 0.0 copy-start.2
  0.0 0.0 copy-start.3
  0.0 0.0 copy-start.1
  0.0 0.9 %copy-done.2 = bf16[8,24,128]{2,1,0:T(8,128)(2,1)S(1)} copy-done((bf16[8,24,128]{2,1,0:T(8,128)(2,1)S(1)}, bf16[8,24,128]{2,1,0:T(8,128)(2,1)}, u32[]{:S(2)}) %copy-start.2) | copy-done | bytes 49176
  1.0 27.3 %all_gather.3.coefficients_ref = bf16[8,384,128]{2,1,0:T(8,128)(2,1)S(1)} all-gather(bf16[8,24,128]{2,1,0:T(8,128)(2,1)S(1)} %copy-done.2), channel_id=1, replica_groups=mesh['wave'=48,'lat'=16] {'lat'}, dimensions={1}, use_global_device_ids=true | all-gather | bytes 835584 | tf_op jit(solution)/shard_map/all_gather | solution.py:153
  28.2 0.0 copy-done.3
  28.2 0.0 copy-done.1
  28.3 0.6 %legendre_sums.1 = (bf16[48,2,8,128]{3,2,1,0:T(8,128)(2,1)S(1)}, bf16[384,512]{1,0:T(8,128)(2,1)S(1)}) custom-call(s32[1,384]{1,0:T(1,128)S(1)} %reshape.3.assignment_ref, s32[1,384]{1,0:T(1,128)S(1)} %degree_row.1.degree_ref, bf16[8,96,384]{2,1,0:T(8,128)(2,1)S(1)} %bitcast.1, bf16[8,384,128]{2,1,0:T(8,128)(2,1)S(1)} %all_gather.3.coefficients_ref), custom_call_target="tpu_custom_call" | custom-call | tf_op jit(solution)/shard_map/legendre_sums/pallas_call | solution.py:72
  28.9 26.3 %all_to_all.5.spectra_ref = bf16[48,2,8,128]{3,2,1,0:T(8,128)(2,1)S(1)} all-to-all(bf16[48,2,8,128]{3,2,1,0:T(8,128)(2,1)S(1)} %get-tuple-element.15), channel_id=1, replica_groups=mesh['wave'=48,'lat'=16] {'wave'}, dimensions={0} | all-to-all | bytes 393216 | tf_op jit(solution)/shard_map/all_to_all | solution.py:156
  55.2 0.0 copy-done
  55.2 2.2 %synthesis.1 = f32[1,2,64,5120]{3,2,1,0:T(8,128)} custom-call(bf16[48,2,8,128]{3,2,1,0:T(8,128)(2,1)S(1)} %all_to_all.5.spectra_ref, bf16[384,512]{1,0:T(8,128)(2,1)S(1)} %get-tuple-element.16.place_ref, bf16[1024,1280]{1,0:T(8,128)(2,1)S(1)} %copy-done), custom_call_target="tpu_custom_call" | custom-call | flops 1000000000 | bytes 6000000 | tf_op jit(solution)/shard_map/synthesis/pallas_call | solution.py:135
  (2 shorter events, 0.0 us)
Async XLA Ops:
  0.0 55.2 %copy-start = (bf16[1024,1280]{1,0:T(8,128)(2,1)S(1)}, bf16[1024,1280]{1,0:T(8,128)(2,1)}, u32[]{:S(2)}) copy-start(bf16[1024,1280]{1,0:T(8,128)(2,1)} %constant.2.clone.table_ref) | copy-start | bytes 7864324
  0.0 0.9 %copy-start.2 = (bf16[8,24,128]{2,1,0:T(8,128)(2,1)S(1)}, bf16[8,24,128]{2,1,0:T(8,128)(2,1)}, u32[]{:S(2)}) copy-start(bf16[8,24,128]{2,1,0:T(8,128)(2,1)} %param.5) | copy-start | bytes 147460
  0.0 28.2 %copy-start.3 = (s32[384]{0:T(512)S(1)}, s32[384]{0:T(512)}, u32[]{:S(2)}) copy-start(s32[384]{0:T(512)} %param.6) | copy-start | bytes 4612
  0.0 28.2 %copy-start.1 = (bf16[8,384,96]{1,2,0:T(8,128)(2,1)S(1)}, bf16[8,384,96]{1,2,0:T(8,128)(2,1)}, u32[]{:S(2)}) copy-start(bf16[8,384,96]{1,2,0:T(8,128)(2,1)} %param.4) | copy-start | bytes 1769476

commit v4 on v3

--- a/solution.py
+++ b/solution.py
@@ -13,6 +13,7 @@
 LANES = 128
 CHUNK = 256
 BLOCK_OF_CLASS = (0, 2, 1, 3)
+WAVE_FIRST = 34
 
 
 def synthesis_table(first, rows):
@@ -28,19 +29,24 @@
     return jnp.asarray(table.reshape(-1, QUARTER).astype(jnp.bfloat16))
 
 
-def degrees_kernel(out_ref):
+def degrees_kernel(_, out_ref):
     out_ref[...] = lax.broadcasted_iota(jnp.int32, out_ref.shape, 1)
 
 
-def degree_row(count):
+def degree_row(count, after):
     return pl.pallas_call(
         degrees_kernel,
         out_shape=jax.ShapeDtypeStruct((1, count), jnp.int32),
+        in_specs=[pl.BlockSpec(memory_space=pl.ANY)],
         out_specs=pl.BlockSpec(memory_space=pltpu.VMEM),
         cost_estimate=pl.CostEstimate(flops=10 ** 9, bytes_accessed=4 * count, transcendentals=0),
         compiler_params=pltpu.CompilerParams(vmem_limit_bytes=2 ** 20),
         name="degree_row",
-    )()
+    )(after)
+
+
+def wave_order(count):
+    return [(WAVE_FIRST + i) % count for i in range(count)]
 
 
 def fields_kernel(assignment_ref, degree_ref, legendre_ref, coefficients_ref, out_ref, place_ref, by_latitude):
@@ -56,9 +62,13 @@
         by_latitude[pl.ds(row, lat_count, stride=row_count), :] = jnp.dot(
             legendre_ref[row] * mask, coefficients_ref[row], preferred_element_type=jnp.float32
         )
-    out_ref[...] = by_latitude[...].astype(out_ref.dtype).reshape(out_ref.shape)
+    wave_count, size = out_ref.shape[:2]
+    order = wave_order(wave_count)
+    for block, wave in enumerate(order):
+        out_ref[block] = by_latitude[wave * size:(wave + 1) * size, :].astype(out_ref.dtype)
     classes = len(BLOCK_OF_CLASS)
     slab = jnp.broadcast_to(slab, (LANES, all_rows)).T
+    slab = jnp.concatenate([slab[wave * row_count:(wave + 1) * row_count] for wave in order], axis=0)
     kind = slab % classes
     block = jnp.where(kind == 1, 2, jnp.where(kind == 2, 1, kind))
     target = block * LANES + slab // classes - lax.broadcasted_iota(jnp.int32, slab.shape, 1)
@@ -72,7 +82,7 @@
     return pl.pallas_call(
         fields_kernel,
         out_shape=(
-            jax.ShapeDtypeStruct((wave_count, lat_count // wave_count, row_count, columns), jnp.bfloat16),
+            jax.ShapeDtypeStruct((wave_count, lat_count // wave_count * row_count, columns), jnp.bfloat16),
             jax.ShapeDtypeStruct((assignment.shape[0], len(BLOCK_OF_CLASS) * LANES), jnp.bfloat16),
         ),
         in_specs=[pl.BlockSpec(memory_space=pltpu.VMEM)] * 4,
@@ -84,13 +94,16 @@
 
 
 def synthesis_kernel(spectra_ref, place_ref, table_ref, out_ref, buffer, semaphore):
-    items = spectra_ref.shape[1]
+    wave_count, size = spectra_ref.shape[:2]
     rows, padded = place_ref.shape
+    row_count = rows // wave_count
+    items = size // row_count
+    spectra = spectra_ref[...].astype(jnp.float32)
     placed = []
     for i in range(items):
-        spectra = spectra_ref[:, i].astype(jnp.float32).reshape(rows, 2 * C).astype(jnp.bfloat16)
+        item = spectra[:, i * row_count:(i + 1) * row_count].reshape(rows, 2 * C).astype(jnp.bfloat16)
         placed.append(lax.dot_general(
-            spectra, place_ref[...], (((0,), (0,)), ((), ())), preferred_element_type=jnp.float32
+            item, place_ref[...], (((0,), (0,)), ((), ())), preferred_element_type=jnp.float32
         ).astype(jnp.bfloat16))
 
     def part(half, item, block):
@@ -130,7 +143,7 @@
 
 
 def synthesis(spectra, place, table):
-    items = spectra.shape[1]
+    items = spectra.shape[0] * spectra.shape[1] // place.shape[0]
     chunks = QUARTER // CHUNK
     return pl.pallas_call(
         synthesis_kernel,
@@ -149,11 +162,13 @@
 
 def shards(legendre, coefficients, assignment):
     wave_count = lax.axis_size("wave")
-    coefficients, degree = lax.optimization_barrier((coefficients, degree_row(legendre.shape[1])))
     gathered = lax.all_gather(coefficients, "lat", axis=1, tiled=True)
-    gathered, assignment = lax.optimization_barrier((gathered, assignment))
+    degree = degree_row(legendre.shape[1], gathered)
+    degree, assignment = lax.optimization_barrier((degree, assignment))
     by_dest, place = legendre_sums(assignment, degree, jnp.swapaxes(legendre, 1, 2), gathered, wave_count)
-    exchanged = lax.all_to_all(by_dest, "wave", split_axis=0, concat_axis=0, tiled=True)
+    exchanged = lax.all_to_all(
+        by_dest, "wave", split_axis=0, concat_axis=0, tiled=True, axis_index_groups=[wave_order(wave_count)]
+    )
     table = synthesis_table(MTOP - assignment.shape[0] + 1, assignment.shape[0])
     return synthesis(exchanged, place, table)
 

time: 57.5 us -> 53 us (0.922)
  blocking collectives: 53.6 us -> 50 us
  local copies, waits for them, and re-layouts: 0.93 us -> 0.01 us
    all_to_all x1, blocking collectives: 26.3 us -> 22.5 us  [shards(): lax.all_to_all(by_dest, 'wave', split_axis=0, concat_axis=0, tiled=True,...]
    unnamed x8 -> x6, local copies, waits for them, and re-layouts: 0.93 us -> 0.01 us
where the time goes in v4:
time: 53 us; the launch traced here: 52.9 us
  blocking collectives  50 us (94%)
  Pallas kernels  2.78 us (5%)
    all_gather x1, blocking collectives, shards(): gathered = lax.all_gather(coefficients, 'lat', axis=1, tiled=True)  27.6 us
    all_to_all x1, blocking collectives, shards(): lax.all_to_all(by_dest, 'wave', split_axis=0, concat_axis=0, tiled=True,...  22.5 us
    pallas_call x1, Pallas kernels, synthesis(): pl.pallas_call(synthesis_kernel, out_shape=jax.ShapeDtypeStruct((1, items...  2.18 us

profile of v4, /device:TPU:1, one launch (start us, length us, event | category | flops | bytes accessed | tf_op | source)
XLA Modules:
  0.0 52.9 jit_solution(15393907765407437900)
XLA Ops:
  0.0 0.0 copy-start.2
  0.0 0.0 copy-start.1
  0.0 27.6 %all_gather.3._.coefficients_ref = bf16[8,384,128]{2,1,0:T(8,128)(2,1)S(1)} all-gather(bf16[8,24,128]{2,1,0:T(8,128)(2,1)} %param.5), channel_id=1, replica_groups=mesh['wave'=48,'lat'=16] {'lat'}, dimensions={1}, use_global_device_ids=true | all-gather | bytes 835584 | tf_op jit(solution)/shard_map/all_gather | solution.py:165
  27.6 0.0 copy-start
  27.6 0.0 copy-done.2
  27.6 0.0 copy-done.1
  27.6 0.6 %legendre_sums.1 = (bf16[48,16,128]{2,1,0:T(8,128)(2,1)S(1)}, bf16[384,512]{1,0:T(8,128)(2,1)S(1)}) custom-call(s32[1,384]{1,0:T(1,128)S(1)} %reshape.3.assignment_ref, s32[1,384]{1,0:T(1,128)S(1)} %degree_row.1.degree_ref, bf16[8,96,384]{2,1,0:T(8,128)(2,1)S(1)} %bitcast.1, bf16[8,384,128]{2,1,0:T(8,128)(2,1)S(1)} %all_gather.3._.coefficients_ref), custom_call_target="tpu_custom_call" | custom-call | tf_op jit(solution)/shard_map/legendre_sums/pallas_call | solution.py:82
  28.2 22.5 %all_to_all.5.spectra_ref = bf16[48,16,128]{2,1,0:T(8,128)(2,1)S(1)} all-to-all(bf16[48,16,128]{2,1,0:T(8,128)(2,1)S(1)} %get-tuple-element.11), channel_id=1, replica_groups={{544,560,576,592,608,624,640,656,672,688,704,720,736,752,0,16,32,48,64,..., dimensions={0} | all-to-all | bytes 393216 | tf_op jit(solution)/shard_map/all_to_all | solution.py:169
  50.7 0.0 copy-done
  50.7 2.2 %synthesis.1 = f32[1,2,64,5120]{3,2,1,0:T(8,128)} custom-call(bf16[48,16,128]{2,1,0:T(8,128)(2,1)S(1)} %all_to_all.5.spectra_ref, bf16[384,512]{1,0:T(8,128)(2,1)S(1)} %get-tuple-element.12.place_ref, bf16[1024,1280]{1,0:T(8,128)(2,1)S(1)} %copy-done), custom_call_target="tpu_custom_call" | custom-call | flops 1000000000 | bytes 6000000 | tf_op jit(solution)/shard_map/synthesis/pallas_call | solution.py:148
  (2 shorter events, 0.0 us)
Async XLA Ops:
  0.0 27.6 %copy-start.2 = (s32[384]{0:T(512)S(1)}, s32[384]{0:T(512)}, u32[]{:S(2)}) copy-start(s32[384]{0:T(512)} %param.6) | copy-start | bytes 4612
  0.0 27.6 %copy-start.1 = (bf16[8,384,96]{1,2,0:T(8,128)(2,1)S(1)}, bf16[8,384,96]{1,2,0:T(8,128)(2,1)}, u32[]{:S(2)}) copy-start(bf16[8,384,96]{1,2,0:T(8,128)(2,1)} %param.4) | copy-start | bytes 1769476
  27.6 23.1 %copy-start = (bf16[1024,1280]{1,0:T(8,128)(2,1)S(1)}, bf16[1024,1280]{1,0:T(8,128)(2,1)}, u32[]{:S(2)}) copy-start(bf16[1024,1280]{1,0:T(8,128)(2,1)} %constant.2.clone.table_ref) | copy-start | bytes 7864324

commit v5 on v4

--- a/solution.py
+++ b/solution.py
@@ -13,7 +13,8 @@
 LANES = 128
 CHUNK = 256
 BLOCK_OF_CLASS = (0, 2, 1, 3)
-WAVE_FIRST = 34
+X_ORDER = (2, 0, 3, 1)
+Z_ORDER = (10, 11, 5, 6, 0, 1, 2, 3, 4, 7, 8, 9)
 
 
 def synthesis_table(first, rows):
@@ -46,7 +47,9 @@
 
 
 def wave_order(count):
-    return [(WAVE_FIRST + i) % count for i in range(count)]
+    order = [len(Z_ORDER) * x + z for x in X_ORDER for z in Z_ORDER]
+    assert sorted(order) == list(range(count))
+    return order
 
 
 def fields_kernel(assignment_ref, degree_ref, legendre_ref, coefficients_ref, out_ref, place_ref, by_latitude):

time: 53 us -> 51.7 us (0.975)
  the two profiles are of different devices: /device:TPU:1 before, /device:TPU:4 now
where the time goes in v5:
time: 51.7 us; the launch traced here: 51.5 us
  blocking collectives  48.7 us (94%)
  Pallas kernels  2.78 us (5%)
    all_to_all x1, blocking collectives, shards(): lax.all_to_all(by_dest, 'wave', split_axis=0, concat_axis=0, tiled=True,...  28.6 us
    all_gather x1, blocking collectives, shards(): gathered = lax.all_gather(coefficients, 'lat', axis=1, tiled=True)  20.1 us
    pallas_call x1, Pallas kernels, synthesis(): pl.pallas_call(synthesis_kernel, out_shape=jax.ShapeDtypeStruct((1, items...  2.18 us

profile of v5, /device:TPU:4, one launch (start us, length us, event | category | flops | bytes accessed | tf_op | source)
XLA Modules:
  0.0 51.5 jit_solution(3310784704650456864)
XLA Ops:
  0.0 0.0 copy-start.2
  0.0 0.0 copy-start.1
  0.0 20.1 %all_gather.3._.coefficients_ref = bf16[8,384,128]{2,1,0:T(8,128)(2,1)S(1)} all-gather(bf16[8,24,128]{2,1,0:T(8,128)(2,1)} %param.5), channel_id=1, replica_groups=mesh['wave'=48,'lat'=16] {'lat'}, dimensions={1}, use_global_device_ids=true | all-gather | bytes 835584 | tf_op jit(solution)/shard_map/all_gather | solution.py:168
  20.1 0.0 copy-start
  20.1 0.0 copy-done.2
  20.1 0.0 copy-done.1
  20.1 0.6 %legendre_sums.1 = (bf16[48,16,128]{2,1,0:T(8,128)(2,1)S(1)}, bf16[384,512]{1,0:T(8,128)(2,1)S(1)}) custom-call(s32[1,384]{1,0:T(1,128)S(1)} %reshape.3.assignment_ref, s32[1,384]{1,0:T(1,128)S(1)} %degree_row.1.degree_ref, bf16[8,96,384]{2,1,0:T(8,128)(2,1)S(1)} %bitcast.1, bf16[8,384,128]{2,1,0:T(8,128)(2,1)S(1)} %all_gather.3._.coefficients_ref), custom_call_target="tpu_custom_call" | custom-call | tf_op jit(solution)/shard_map/legendre_sums/pallas_call | solution.py:85
  20.7 28.6 %all_to_all.5.spectra_ref = bf16[48,16,128]{2,1,0:T(8,128)(2,1)S(1)} all-to-all(bf16[48,16,128]{2,1,0:T(8,128)(2,1)S(1)} %get-tuple-element.11), channel_id=1, replica_groups={{544,560,464,480,384,400,416,432,448,496,512,528,160,176,80,96,0,16,32,..., dimensions={0} | all-to-all | bytes 393216 | tf_op jit(solution)/shard_map/all_to_all | solution.py:172
  49.4 0.0 copy-done
  49.4 2.2 %synthesis.1 = f32[1,2,64,5120]{3,2,1,0:T(8,128)} custom-call(bf16[48,16,128]{2,1,0:T(8,128)(2,1)S(1)} %all_to_all.5.spectra_ref, bf16[384,512]{1,0:T(8,128)(2,1)S(1)} %get-tuple-element.12.place_ref, bf16[1024,1280]{1,0:T(8,128)(2,1)S(1)} %copy-done), custom_call_target="tpu_custom_call" | custom-call | flops 1000000000 | bytes 6000000 | tf_op jit(solution)/shard_map/synthesis/pallas_call | solution.py:151
  (2 shorter events, 0.0 us)
Async XLA Ops:
  0.0 20.1 %copy-start.2 = (s32[384]{0:T(512)S(1)}, s32[384]{0:T(512)}, u32[]{:S(2)}) copy-start(s32[384]{0:T(512)} %param.6) | copy-start | bytes 4612
  0.0 20.1 %copy-start.1 = (bf16[8,384,96]{1,2,0:T(8,128)(2,1)S(1)}, bf16[8,384,96]{1,2,0:T(8,128)(2,1)}, u32[]{:S(2)}) copy-start(bf16[8,384,96]{1,2,0:T(8,128)(2,1)} %param.4) | copy-start | bytes 1769476
  20.1 29.2 %copy-start = (bf16[1024,1280]{1,0:T(8,128)(2,1)S(1)}, bf16[1024,1280]{1,0:T(8,128)(2,1)}, u32[]{:S(2)}) copy-start(bf16[1024,1280]{1,0:T(8,128)(2,1)} %constant.2.clone.table_ref) | copy-start | bytes 7864324

commit v6 on v5

--- a/solution.py
+++ b/solution.py
@@ -56,25 +56,25 @@
     row_count, lat_count, deg_count = legendre_ref.shape
     all_rows = assignment_ref.shape[1]
     first_row = lax.axis_index("wave") * row_count
-    place = lax.broadcasted_iota(jnp.int32, (1, all_rows), 1)
-    degree = degree_ref[...]
+    row = lax.broadcasted_iota(jnp.int32, (row_count, all_rows), 0)
+    place = lax.broadcasted_iota(jnp.int32, (row_count, all_rows), 1)
     slab = assignment_ref[...]
+    own = jnp.sum(jnp.where(place == first_row + row, slab, 0), axis=1, keepdims=True)
+    masks = jnp.where(degree_ref[...] < all_rows - own, 1.0, 0.0).astype(jnp.bfloat16)
     for row in range(row_count):
-        own = jnp.sum(jnp.where(place == first_row + row, slab, 0), axis=1, keepdims=True)
-        mask = jnp.where(degree < all_rows - own, 1.0, 0.0).astype(jnp.bfloat16)
         by_latitude[pl.ds(row, lat_count, stride=row_count), :] = jnp.dot(
-            legendre_ref[row] * mask, coefficients_ref[row], preferred_element_type=jnp.float32
+            legendre_ref[row] * masks[row:row + 1], coefficients_ref[row], preferred_element_type=jnp.float32
         )
     wave_count, size = out_ref.shape[:2]
     order = wave_order(wave_count)
     for block, wave in enumerate(order):
         out_ref[block] = by_latitude[wave * size:(wave + 1) * size, :].astype(out_ref.dtype)
     classes = len(BLOCK_OF_CLASS)
-    slab = jnp.broadcast_to(slab, (LANES, all_rows)).T
-    slab = jnp.concatenate([slab[wave * row_count:(wave + 1) * row_count] for wave in order], axis=0)
     kind = slab % classes
-    block = jnp.where(kind == 1, 2, jnp.where(kind == 2, 1, kind))
-    target = block * LANES + slab // classes - lax.broadcasted_iota(jnp.int32, slab.shape, 1)
+    position = jnp.where(kind == 1, 2, jnp.where(kind == 2, 1, kind))
+    target = jnp.broadcast_to(position * LANES + slab // classes, (LANES, all_rows)).T
+    target = jnp.concatenate([target[wave * row_count:(wave + 1) * row_count] for wave in order], axis=0)
+    target -= lax.broadcasted_iota(jnp.int32, target.shape, 1)
     for n in range(classes):
         place_ref[:, n * LANES:(n + 1) * LANES] = jnp.where(target == n * LANES, 1.0, 0.0).astype(place_ref.dtype)
 
@@ -90,7 +90,7 @@
         ),
         in_specs=[pl.BlockSpec(memory_space=pltpu.VMEM)] * 4,
         out_specs=(pl.BlockSpec(memory_space=pltpu.VMEM), pl.BlockSpec(memory_space=pltpu.VMEM)),
-        scratch_shapes=[pltpu.VMEM((row_count * lat_count, columns), jnp.float32)],
+        scratch_shapes=[pltpu.VMEM((row_count * (lat_count + 1), columns), jnp.float32)],
         compiler_params=pltpu.CompilerParams(vmem_limit_bytes=16 * 2 ** 20),
         name="legendre_sums",
     )(assignment.reshape(1, -1), degree, legendre, coefficients)

time: 51.7 us -> 51.5 us (level)
  no operation moved by 1% of the time
where the time goes in v6:
time: 51.5 us; the launch traced here: 51.4 us
  blocking collectives  48.7 us (95%)
  Pallas kernels  2.64 us (5%)
    all_to_all x1, blocking collectives, shards(): lax.all_to_all(by_dest, 'wave', split_axis=0, concat_axis=0, tiled=True,...  28.6 us
    all_gather x1, blocking collectives, shards(): gathered = lax.all_gather(coefficients, 'lat', axis=1, tiled=True)  20.1 us
    pallas_call x1, Pallas kernels, synthesis(): pl.pallas_call(synthesis_kernel, out_shape=jax.ShapeDtypeStruct((1, items...  2.19 us

profile of v6, /device:TPU:4, one launch (start us, length us, event | category | flops | bytes accessed | tf_op | source)
XLA Modules:
  0.0 51.4 jit_solution(7401843148171825709)
XLA Ops:
  0.0 0.0 copy-start.2
  0.0 0.0 copy-start.1
  0.0 20.1 %all_gather.3._.coefficients_ref = bf16[8,384,128]{2,1,0:T(8,128)(2,1)S(1)} all-gather(bf16[8,24,128]{2,1,0:T(8,128)(2,1)} %param.5), channel_id=1, replica_groups=mesh['wave'=48,'lat'=16] {'lat'}, dimensions={1}, use_global_device_ids=true | all-gather | bytes 835584 | tf_op jit(solution)/shard_map/all_gather | solution.py:168
  20.1 0.0 copy-start
  20.1 0.0 copy-done.2
  20.1 0.0 copy-done.1
  20.1 0.4 legendre_sums.1
  20.6 28.6 %all_to_all.5.spectra_ref = bf16[48,16,128]{2,1,0:T(8,128)(2,1)S(1)} all-to-all(bf16[48,16,128]{2,1,0:T(8,128)(2,1)S(1)} %get-tuple-element.11), channel_id=1, replica_groups={{544,560,464,480,384,400,416,432,448,496,512,528,160,176,80,96,0,16,32,..., dimensions={0} | all-to-all | bytes 393216 | tf_op jit(solution)/shard_map/all_to_all | solution.py:172
  49.2 0.0 copy-done
  49.2 2.2 %synthesis.1 = f32[1,2,64,5120]{3,2,1,0:T(8,128)} custom-call(bf16[48,16,128]{2,1,0:T(8,128)(2,1)S(1)} %all_to_all.5.spectra_ref, bf16[384,512]{1,0:T(8,128)(2,1)S(1)} %get-tuple-element.12.place_ref, bf16[1024,1280]{1,0:T(8,128)(2,1)S(1)} %copy-done), custom_call_target="tpu_custom_call" | custom-call | flops 1000000000 | bytes 6000000 | tf_op jit(solution)/shard_map/synthesis/pallas_call | solution.py:151
  (2 shorter events, 0.0 us)
Async XLA Ops:
  0.0 20.1 %copy-start.2 = (s32[384]{0:T(512)S(1)}, s32[384]{0:T(512)}, u32[]{:S(2)}) copy-start(s32[384]{0:T(512)} %param.6) | copy-start | bytes 4612
  0.0 20.1 %copy-start.1 = (bf16[8,384,96]{1,2,0:T(8,128)(2,1)S(1)}, bf16[8,384,96]{1,2,0:T(8,128)(2,1)}, u32[]{:S(2)}) copy-start(bf16[8,384,96]{1,2,0:T(8,128)(2,1)} %param.4) | copy-start | bytes 1769476
  20.1 29.1 %copy-start = (bf16[1024,1280]{1,0:T(8,128)(2,1)S(1)}, bf16[1024,1280]{1,0:T(8,128)(2,1)}, u32[]{:S(2)}) copy-start(bf16[1024,1280]{1,0:T(8,128)(2,1)} %constant.2.clone.table_ref) | copy-start | bytes 7864324

commit v7 on v6

--- a/solution.py
+++ b/solution.py
@@ -13,6 +13,7 @@
 LANES = 128
 CHUNK = 256
 BLOCK_OF_CLASS = (0, 2, 1, 3)
+Y_ORDER = (0, 7, 6, 5, 4, 3, 2, 1)
 X_ORDER = (2, 0, 3, 1)
 Z_ORDER = (10, 11, 5, 6, 0, 1, 2, 3, 4, 7, 8, 9)
 
@@ -61,9 +62,13 @@
     slab = assignment_ref[...]
     own = jnp.sum(jnp.where(place == first_row + row, slab, 0), axis=1, keepdims=True)
     masks = jnp.where(degree_ref[...] < all_rows - own, 1.0, 0.0).astype(jnp.bfloat16)
+    chip_degrees = deg_count // len(Y_ORDER)
+    starts = [Y_ORDER.index(y) * chip_degrees for y in range(len(Y_ORDER))]
     for row in range(row_count):
         by_latitude[pl.ds(row, lat_count, stride=row_count), :] = jnp.dot(
-            legendre_ref[row] * masks[row:row + 1], coefficients_ref[row], preferred_element_type=jnp.float32
+            legendre_ref[row] * masks[row:row + 1],
+            jnp.concatenate([coefficients_ref[row, start:start + chip_degrees, :] for start in starts], axis=0),
+            preferred_element_type=jnp.float32,
         )
     wave_count, size = out_ref.shape[:2]
     order = wave_order(wave_count)
@@ -165,7 +170,8 @@
 
 def shards(legendre, coefficients, assignment):
     wave_count = lax.axis_size("wave")
-    gathered = lax.all_gather(coefficients, "lat", axis=1, tiled=True)
+    ring = [2 * y + core for y in Y_ORDER for core in range(2)]
+    gathered = lax.all_gather(coefficients, "lat", axis=1, tiled=True, axis_index_groups=[ring])
     degree = degree_row(legendre.shape[1], gathered)
     degree, assignment = lax.optimization_barrier((degree, assignment))
     by_dest, place = legendre_sums(assignment, degree, jnp.swapaxes(legendre, 1, 2), gathered, wave_count)

time: 51.5 us -> 51 us (level)
  the two profiles are of different devices: /device:TPU:4 before, /device:TPU:24 now
where the time goes in v7:
time: 51 us; the launch traced here: 50.9 us
  blocking collectives  48.2 us (95%)
  Pallas kernels  2.64 us (5%)
    all_to_all x1, blocking collectives, shards(): lax.all_to_all(by_dest, 'wave', split_axis=0, concat_axis=0, tiled=True,...  24.4 us
    all_gather x1, blocking collectives, shards(): lax.all_gather(coefficients, 'lat', axis=1, tiled=True, axis_index_groups...  23.8 us
    pallas_call x1, Pallas kernels, synthesis(): pl.pallas_call(synthesis_kernel, out_shape=jax.ShapeDtypeStruct((1, items...  2.19 us

profile of v7, /device:TPU:24, one launch (start us, length us, event | category | flops | bytes accessed | tf_op | source)
XLA Modules:
  0.0 50.9 jit_solution(4891190520178866815)
XLA Ops:
  0.0 0.0 copy-start.2
  0.0 0.0 copy-start.1
  0.0 23.8 %all_gather.3._.coefficients_ref = bf16[8,384,128]{2,1,0:T(8,128)(2,1)S(1)} all-gather(bf16[8,24,128]{2,1,0:T(8,128)(2,1)} %param.5), channel_id=1, replica_groups={{0,1,14,15,12,13,10,11,8,9,6,7,4,5,2,3},{16,17,30,31,28,29,26,27,24,25,..., dimensions={1}, use_global_device_ids=true | all-gather | bytes 835584 | tf_op jit(solution)/shard_map/all_gather | solution.py:174
  23.8 0.0 copy-start
  23.8 0.0 copy-done.2
  23.8 0.0 copy-done.1
  23.8 0.4 legendre_sums.1
  24.3 24.4 %all_to_all.5.spectra_ref = bf16[48,16,128]{2,1,0:T(8,128)(2,1)S(1)} all-to-all(bf16[48,16,128]{2,1,0:T(8,128)(2,1)S(1)} %get-tuple-element.11), channel_id=1, replica_groups={{544,560,464,480,384,400,416,432,448,496,512,528,160,176,80,96,0,16,32,..., dimensions={0} | all-to-all | bytes 393216 | tf_op jit(solution)/shard_map/all_to_all | solution.py:178
  48.7 0.0 copy-done
  48.7 2.2 %synthesis.1 = f32[1,2,64,5120]{3,2,1,0:T(8,128)} custom-call(bf16[48,16,128]{2,1,0:T(8,128)(2,1)S(1)} %all_to_all.5.spectra_ref, bf16[384,512]{1,0:T(8,128)(2,1)S(1)} %get-tuple-element.12.place_ref, bf16[1024,1280]{1,0:T(8,128)(2,1)S(1)} %copy-done), custom_call_target="tpu_custom_call" | custom-call | flops 1000000000 | bytes 6000000 | tf_op jit(solution)/shard_map/synthesis/pallas_call | solution.py:156
  (2 shorter events, 0.0 us)
Async XLA Ops:
  0.0 23.8 %copy-start.2 = (s32[384]{0:T(512)S(1)}, s32[384]{0:T(512)}, u32[]{:S(2)}) copy-start(s32[384]{0:T(512)} %param.6) | copy-start | bytes 4612
  0.0 23.8 %copy-start.1 = (bf16[8,384,96]{1,2,0:T(8,128)(2,1)S(1)}, bf16[8,384,96]{1,2,0:T(8,128)(2,1)}, u32[]{:S(2)}) copy-start(bf16[8,384,96]{1,2,0:T(8,128)(2,1)} %param.4) | copy-start | bytes 1769476
  23.8 24.9 %copy-start = (bf16[1024,1280]{1,0:T(8,128)(2,1)S(1)}, bf16[1024,1280]{1,0:T(8,128)(2,1)}, u32[]{:S(2)}) copy-start(bf16[1024,1280]{1,0:T(8,128)(2,1)} %constant.2.clone.table_ref) | copy-start | bytes 7864324

commit v8 on v7

--- a/solution.py
+++ b/solution.py
@@ -13,7 +13,7 @@
 LANES = 128
 CHUNK = 256
 BLOCK_OF_CLASS = (0, 2, 1, 3)
-Y_ORDER = (0, 7, 6, 5, 4, 3, 2, 1)
+Y_ORDER = (6, 5, 4, 3, 2, 1, 0, 7)
 X_ORDER = (2, 0, 3, 1)
 Z_ORDER = (10, 11, 5, 6, 0, 1, 2, 3, 4, 7, 8, 9)
 

time: 51 us -> 51 us (level)
  no operation moved by 1% of the time
where the time goes in v8:
time: 51 us; the launch traced here: 50.9 us
  blocking collectives  48.2 us (95%)
  Pallas kernels  2.65 us (5%)
    all_to_all x1, blocking collectives, shards(): lax.all_to_all(by_dest, 'wave', split_axis=0, concat_axis=0, tiled=True,...  24.4 us
    all_gather x1, blocking collectives, shards(): lax.all_gather(coefficients, 'lat', axis=1, tiled=True, axis_index_groups...  23.8 us
    pallas_call x1, Pallas kernels, synthesis(): pl.pallas_call(synthesis_kernel, out_shape=jax.ShapeDtypeStruct((1, items...  2.2 us

profile of v8, /device:TPU:24, one launch (start us, length us, event | category | flops | bytes accessed | tf_op | source)
XLA Modules:
  0.0 50.9 jit_solution(17607570984432951976)
XLA Ops:
  0.0 0.0 copy-start.2
  0.0 0.0 copy-start.1
  0.0 23.8 %all_gather.3._.coefficients_ref = bf16[8,384,128]{2,1,0:T(8,128)(2,1)S(1)} all-gather(bf16[8,24,128]{2,1,0:T(8,128)(2,1)} %param.5), channel_id=1, replica_groups={{12,13,10,11,8,9,6,7,4,5,2,3,0,1,14,15},{28,29,26,27,24,25,22,23,20,21,..., dimensions={1}, use_global_device_ids=true | all-gather | bytes 835584 | tf_op jit(solution)/shard_map/all_gather | solution.py:174
  23.8 0.0 copy-start
  23.8 0.0 copy-done.2
  23.8 0.0 copy-done.1
  23.8 0.4 legendre_sums.1
  24.3 24.4 %all_to_all.5.spectra_ref = bf16[48,16,128]{2,1,0:T(8,128)(2,1)S(1)} all-to-all(bf16[48,16,128]{2,1,0:T(8,128)(2,1)S(1)} %get-tuple-element.11), channel_id=1, replica_groups={{544,560,464,480,384,400,416,432,448,496,512,528,160,176,80,96,0,16,32,..., dimensions={0} | all-to-all | bytes 393216 | tf_op jit(solution)/shard_map/all_to_all | solution.py:178
  48.7 0.0 copy-done
  48.7 2.2 %synthesis.1 = f32[1,2,64,5120]{3,2,1,0:T(8,128)} custom-call(bf16[48,16,128]{2,1,0:T(8,128)(2,1)S(1)} %all_to_all.5.spectra_ref, bf16[384,512]{1,0:T(8,128)(2,1)S(1)} %get-tuple-element.12.place_ref, bf16[1024,1280]{1,0:T(8,128)(2,1)S(1)} %copy-done), custom_call_target="tpu_custom_call" | custom-call | flops 1000000000 | bytes 6000000 | tf_op jit(solution)/shard_map/synthesis/pallas_call | solution.py:156
  (2 shorter events, 0.0 us)
Async XLA Ops:
  0.0 23.8 %copy-start.2 = (s32[384]{0:T(512)S(1)}, s32[384]{0:T(512)}, u32[]{:S(2)}) copy-start(s32[384]{0:T(512)} %param.6) | copy-start | bytes 4612
  0.0 23.8 %copy-start.1 = (bf16[8,384,96]{1,2,0:T(8,128)(2,1)S(1)}, bf16[8,384,96]{1,2,0:T(8,128)(2,1)}, u32[]{:S(2)}) copy-start(bf16[8,384,96]{1,2,0:T(8,128)(2,1)} %param.4) | copy-start | bytes 1769476
  23.8 24.9 %copy-start = (bf16[1024,1280]{1,0:T(8,128)(2,1)S(1)}, bf16[1024,1280]{1,0:T(8,128)(2,1)}, u32[]{:S(2)}) copy-start(bf16[1024,1280]{1,0:T(8,128)(2,1)} %constant.2.clone.table_ref) | copy-start | bytes 7864324

commit v9 on v7

--- a/solution.py
+++ b/solution.py
@@ -15,7 +15,8 @@
 BLOCK_OF_CLASS = (0, 2, 1, 3)
 Y_ORDER = (0, 7, 6, 5, 4, 3, 2, 1)
 X_ORDER = (2, 0, 3, 1)
-Z_ORDER = (10, 11, 5, 6, 0, 1, 2, 3, 4, 7, 8, 9)
+Z_ORDER = (5, 6, 0, 1, 2, 3, 4, 7, 8, 9, 10, 11)
+FIRST = 34
 
 
 def synthesis_table(first, rows):
@@ -49,6 +50,7 @@
 
 def wave_order(count):
     order = [len(Z_ORDER) * x + z for x in X_ORDER for z in Z_ORDER]
+    order = order[order.index(FIRST):] + order[:order.index(FIRST)]
     assert sorted(order) == list(range(count))
     return order
 

time: 51 us -> 51 us (level)
  no operation moved by 1% of the time
where the time goes in v9:
time: 51 us; the launch traced here: 50.8 us
  blocking collectives  48.1 us (94%)
  Pallas kernels  2.65 us (5%)
    all_to_all x1, blocking collectives, shards(): lax.all_to_all(by_dest, 'wave', split_axis=0, concat_axis=0, tiled=True,...  24.4 us
    all_gather x1, blocking collectives, shards(): lax.all_gather(coefficients, 'lat', axis=1, tiled=True, axis_index_groups...  23.8 us
    pallas_call x1, Pallas kernels, synthesis(): pl.pallas_call(synthesis_kernel, out_shape=jax.ShapeDtypeStruct((1, items...  2.21 us

profile of v9, /device:TPU:24, one launch (start us, length us, event | category | flops | bytes accessed | tf_op | source)
XLA Modules:
  0.0 50.8 jit_solution(3837801676711332027)
XLA Ops:
  0.0 0.0 copy-start.2
  0.0 0.0 copy-start.1
  0.0 23.8 %all_gather.3._.coefficients_ref = bf16[8,384,128]{2,1,0:T(8,128)(2,1)S(1)} all-gather(bf16[8,24,128]{2,1,0:T(8,128)(2,1)} %param.5), channel_id=1, replica_groups={{0,1,14,15,12,13,10,11,8,9,6,7,4,5,2,3},{16,17,30,31,28,29,26,27,24,25,..., dimensions={1}, use_global_device_ids=true | all-gather | bytes 835584 | tf_op jit(solution)/shard_map/all_gather | solution.py:176
  23.8 0.0 copy-start
  23.8 0.0 copy-done.2
  23.8 0.0 copy-done.1
  23.8 0.4 legendre_sums.1
  24.3 24.4 %all_to_all.5.spectra_ref = bf16[48,16,128]{2,1,0:T(8,128)(2,1)S(1)} all-to-all(bf16[48,16,128]{2,1,0:T(8,128)(2,1)S(1)} %get-tuple-element.11), channel_id=1, replica_groups={{544,560,80,96,0,16,32,48,64,112,128,144,160,176,656,672,576,592,608,62..., dimensions={0} | all-to-all | bytes 393216 | tf_op jit(solution)/shard_map/all_to_all | solution.py:180
  48.6 0.0 copy-done
  48.6 2.2 %synthesis.1 = f32[1,2,64,5120]{3,2,1,0:T(8,128)} custom-call(bf16[48,16,128]{2,1,0:T(8,128)(2,1)S(1)} %all_to_all.5.spectra_ref, bf16[384,512]{1,0:T(8,128)(2,1)S(1)} %get-tuple-element.12.place_ref, bf16[1024,1280]{1,0:T(8,128)(2,1)S(1)} %copy-done), custom_call_target="tpu_custom_call" | custom-call | flops 1000000000 | bytes 6000000 | tf_op jit(solution)/shard_map/synthesis/pallas_call | solution.py:158
  (2 shorter events, 0.0 us)
Async XLA Ops:
  0.0 23.8 %copy-start.2 = (s32[384]{0:T(512)S(1)}, s32[384]{0:T(512)}, u32[]{:S(2)}) copy-start(s32[384]{0:T(512)} %param.6) | copy-start | bytes 4612
  0.0 23.8 %copy-start.1 = (bf16[8,384,96]{1,2,0:T(8,128)(2,1)S(1)}, bf16[8,384,96]{1,2,0:T(8,128)(2,1)}, u32[]{:S(2)}) copy-start(bf16[8,384,96]{1,2,0:T(8,128)(2,1)} %param.4) | copy-start | bytes 1769476
  23.8 24.8 %copy-start = (bf16[1024,1280]{1,0:T(8,128)(2,1)S(1)}, bf16[1024,1280]{1,0:T(8,128)(2,1)}, u32[]{:S(2)}) copy-start(bf16[1024,1280]{1,0:T(8,128)(2,1)} %constant.2.clone.table_ref) | copy-start | bytes 7864324
